TPU v7x, 32 devices: a whole 2x2x4 slice. The times are simulated.
32 devices in a mesh: groups: 2 (over y), tm: 16 (over z, x, core).
Axes of the slice: x: 2, y: 2, z: 4, core: 2. Of those that a mesh axis runs over, the one named last changes fastest.
Arguments:
- voltages: bfloat16 [256, 256, 2, 188], P(None, ('groups', 'tm')), parts along dimension 1, as said below
- off_starts: int32 [16], P('groups'), parts along dimension 0, may hold values from 0 to 124, as said below
- pointing: int32 [36], replicated, may hold values from 0 to 2047, as said below
- patterns: bfloat16 [2, 188, 2048], P(None, None, 'tm'), may hold values from -0.3125 to 0.3125
Outputs:
- beam_weights: bfloat16 [512, 2, 6768], P(('groups', 'tm')), parts along dimension 0
- beam_maps: float32 [512, 36, 2048], P('groups', None, 'tm'), parts along dimension 0
There are 2 independent parts, one for each index of `groups`. A program takes and returns all parts, laid end to end along the dimension named above; an argument that names none is the same for every part. Nothing has to cross between parts.
Inputs may be any that keep to these rules, and one draw needn't show every extreme that they name: Complex port voltages: thermal noise whose power differs between ports and grows along time, plus sky signals common to the ports. `off_starts`: each of the 8 off-source ranges covers 4 samples from this start; ranges may intersect. `pointing`: several beams may point at the same pixel.
All inputs are finite; a program needn't handle non-finite values.
Results may differ from a plain program's by a relative error of at most 0.0034.
Values may be sent and summed in bfloat16 or wider, within the bound.
A program may use at most 64 MiB of HBM per device.

v0:
```python
import jax
import jax.numpy as jnp
from jax import lax
from jax.sharding import PartitionSpec as P

ITERS = 20


highest = lax.Precision.HIGHEST


def off_flags(moments, starts, range_len):
    shape_now = moments.shape
    flat_moments = moments.reshape(-1)
    inside = (flat_moments[None, :] >= starts[:, None]) & (
        flat_moments[None, :] < starts[:, None] + range_len
    )
    return jnp.any(inside, axis=0).reshape(shape_now)


def split_gram(products, port_count):
    corr_real = products[..., :port_count, :port_count] + products[..., port_count:, port_count:]
    corr_imag = products[..., port_count:, :port_count] - products[..., :port_count, port_count:]
    return jnp.stack([corr_real, corr_imag], axis=-3)


def beam_power(weights, patterns):
    port_count = weights.shape[3]
    real_rows = jnp.concatenate([weights[:, 0], weights[:, 1]], axis=-1)
    imag_rows = jnp.concatenate([-weights[:, 1], weights[:, 0]], axis=-1)
    rows_all = jnp.stack([real_rows, imag_rows], axis=2).reshape(-1, 2 * port_count)
    response = jnp.dot(
        rows_all, patterns.reshape(2 * port_count, -1), preferred_element_type=jnp.float32
    )
    response = response.reshape(weights.shape[0], weights.shape[2], 2, -1)
    return response[:, :, 0] * response[:, :, 0] + response[:, :, 1] * response[:, :, 1]


def on_device(voltages, off_starts, pointing, patterns):
    devices = lax.axis_size("tm")
    position = lax.axis_index("tm")
    channels = voltages.shape[0]
    samples_dev = voltages.shape[1]
    ports = voltages.shape[3]
    beams = pointing.shape[0]
    per_dev = channels // devices
    double_width = 2 * ports
    total_time = samples_dev * devices
    off_span = max(4, total_time // 32)
    every_moment = jnp.arange(total_time, dtype=jnp.int32)
    off_count = jnp.sum(off_flags(every_moment, off_starts, off_span).astype(jnp.float32))
    pixels = patterns.shape[2]
    pixel_ids = position * pixels + jnp.arange(pixels, dtype=jnp.int32)
    selector = (pixel_ids[:, None] == pointing[None, :]).astype(jnp.bfloat16)
    steer_local = jnp.einsum("rpx,xb->rpb", patterns, selector, preferred_element_type=jnp.float32)
    steering = lax.psum(steer_local, "tm")
    blocks = voltages.reshape(devices, per_dev, samples_dev, double_width)
    arrived = lax.all_to_all(blocks, "tm", split_axis=0, concat_axis=0, tiled=True)
    moments = (
        jnp.arange(devices, dtype=jnp.int32)[:, None] * samples_dev
        + jnp.arange(samples_dev, dtype=jnp.int32)[None, :]
    )
    is_off = off_flags(moments, off_starts, off_span)
    on_source = jnp.where(is_off[:, None, :, None], jnp.zeros_like(arrived), arrived)
    products = jnp.einsum("nksi,nksj->kij", on_source, arrived, preferred_element_type=jnp.float32)
    corr_mine = split_gram(products, ports)
    squared = jnp.square(arrived.astype(jnp.float32))
    powers = jnp.sum(jnp.where(is_off[:, None, :, None], squared, jnp.float32(0.0)), axis=(0, 2))
    noise_total = powers[:, :ports] + powers[:, ports:]
    noise_power = noise_total / off_count + 1e-06
    scales = 1.0 / jnp.sqrt(noise_power)
    white_real = corr_mine[:, 0] * scales[:, :, None] * scales[:, None, :]
    white_imag = corr_mine[:, 1] * scales[:, :, None] * scales[:, None, :]
    steer_real = steering[0][None]
    steer_imag = steering[1][None]

    def apply_white(matrix, vector):
        return jnp.einsum("kij,kjb->kib", matrix, vector, precision=highest)

    def power_turn(counter, state_pair):
        beam_real, beam_imag = state_pair
        conj_real = steer_real * beam_real + steer_imag * beam_imag
        conj_imag = steer_real * beam_imag - steer_imag * beam_real
        mixed_real = apply_white(white_real, conj_real) - apply_white(white_imag, conj_imag)
        mixed_imag = apply_white(white_real, conj_imag) + apply_white(white_imag, conj_real)
        image_real = steer_real * mixed_real - steer_imag * mixed_imag
        image_imag = steer_real * mixed_imag + steer_imag * mixed_real
        mean_square = (
            jnp.sum(image_real * image_real, axis=1) + jnp.sum(image_imag * image_imag, axis=1)
        ) / (2 * ports)
        factor = 1.0 / jnp.sqrt(mean_square + 1e-06)
        return (image_real * factor[:, None, :], image_imag * factor[:, None, :])

    initial = (
        jnp.broadcast_to(steer_real, (per_dev, ports, beams)),
        jnp.broadcast_to(steer_imag, (per_dev, ports, beams)),
    )
    beam_real, beam_imag = lax.fori_loop(0, ITERS, power_turn, initial)
    weight_real = beam_real * scales[:, :, None]
    weight_imag = beam_imag * scales[:, :, None]
    weight_pair = (
        jnp.stack([weight_real, weight_imag], axis=1).transpose(0, 1, 3, 2).astype(jnp.bfloat16)
    )
    flat_pair = weight_pair.reshape(per_dev, 2, beams * ports)
    collected = lax.all_gather(flat_pair, "tm", axis=0, tiled=True)
    all_weights = collected.reshape(channels, 2, beams, ports)
    maps_out = beam_power(all_weights, patterns)
    return (flat_pair, maps_out)


def solution(mesh):
    in_specs = (P(None, ("groups", "tm"), None, None), P("groups"), P(), P(None, None, "tm"))
    out_specs = (P(("groups", "tm"), None, None), P("groups", None, "tm"))
    return jax.shard_map(
        on_device, mesh=mesh, in_specs=in_specs, out_specs=out_specs, check_vma=False
    )
```

profile of v0, /device:TPU:29, one launch (start us, length us, event | category | flops | bytes accessed | tf_op | source)
XLA Modules:
  0.0 550.3 jit_solution(12295495400840213857)
XLA Ops:
  7.2 7.9 %copy.28 = bf16[256,8,2,188]{3,2,1,0:T(2,128)(2,1)S(1)} copy(bf16[256,8,2,188]{0,2,3,1:T(2,128)(2,1)} %param.6) | data formatting | bytes 3080192 | tf_op args[0]
  17.1 6.4 %all-to-all-start = ((bf16[16,16,8,376]{3,2,1,0:T(8,128)(2,1)}), bf16[16,16,8,376]{3,2,1,0:T(8,128)(2,1)S(1)}, u32[]{:S(2)}, u32[]{:S(2)}) async-start(bf16[16,16,8,376]{3,2,1,0:T(8,128)(2,1)} %reshape.61), calls=%async_computation | async-start | bytes 3145728 | tf_op jit(solution)/shard_map/all_to_all | solution.py:58
  24.1 74.0 %psum.7 = f32[2,188,36]{1,2,0:T(8,128)S(1)} all-reduce(f32[2,188,36]{1,2,0:T(8,128)S(1)} %convolution_bitcast_fusion.1), channel_id=1, replica_groups=mesh['groups'=2,'tm'=16] {'tm'}, use_global_device_ids=true, to_apply=%region_0.0 | all-reduce | flops 13536 | bytes 108288 | tf_op jit(solution)/shard_map/psum | solution.py:56
  101.8 3.6 fusion.11
  107.1 321.7 %while.12 = (s32[]{:T(128)}, f32[16,188,36]{1,2,0:T(8,128)}, f32[16,188,36]{1,2,0:T(8,128)}, f32[1,188,36]{1,2,0:T(8,128)S(1)}, f32[1,188,36]{1,2,0:T(8,128)S(1)...) while((s32[]{:T(128)}, f32[16,188,36]{1,2,0:T(8,128)}, f32[16,188,36]{1,2,0:T(8,128)}, ...), condition=%wide.region_8.9_spmd, body=%wide.region_5.8_spmd.sunk | while | flops 980656704 | bytes 30075944 | solution.py:98
  107.1 5.4 fusion.50
  118.7 3.2 multiply_reduce_fusion.3
  123.2 5.4 fusion.50
  139.3 5.4 fusion.50
  155.4 5.4 fusion.50
  171.5 5.4 fusion.50
  187.6 5.4 fusion.50
  203.6 5.4 fusion.50
  219.7 5.4 fusion.50
  235.8 5.4 fusion.50
  251.9 5.4 fusion.50
  268.0 5.4 fusion.50
  284.1 5.4 fusion.50
  300.1 5.4 fusion.50
  316.2 5.4 fusion.50
  332.3 5.4 fusion.50
  348.4 5.4 fusion.50
  364.5 5.4 fusion.50
  380.6 5.4 fusion.50
  396.7 5.4 fusion.50
  412.7 5.4 fusion.50
  433.8 67.1 %all-gather.2.cloned.1.call-done = bf16[256,2,6768]{2,0,1:T(8,128)(2,1)} async-done(((bf16[16,2,6768]{2,0,1:T(8,128)(2,1)}), bf16[256,2,6768]{2,0,1:T(8,128)(2,1)}) %all-gather.2.cloned.1.call-update) | async-done | bytes 6930448 | tf_op jit(solution)/shard_map/all_gather | solution.py:105
  500.9 10.1 %copy.29 = bf16[256,2,6768]{0,2,1:T(8,128)(2,1)} copy(bf16[256,2,6768]{2,0,1:T(8,128)(2,1)} %all-gather.2.cloned.1.call-done) | data formatting | bytes 13860864 | tf_op jit(solution)/shard_map/all_gather | solution.py:105
  511.1 9.9 %reshape.63 = bf16[256,2,36,188]{0,3,2,1:T(8,128)(2,1)} reshape(bf16[256,2,6768]{0,2,1:T(8,128)(2,1)} %copy.29) | data formatting | bytes 13860864 | tf_op jit(solution)/shard_map/reshape | solution.py:106
  521.0 3.7 slice_bitcast_fusion
  526.3 7.0 %maximum_bitcast_fusion = (bf16[256,36,1,376]{0,3,2,1:T(8,128)(2,1)}, bf16[256,36,1,376]{0,3,2,1:T(8,128)(2,1)}) fusion(bf16[256,36,188]{0,2,1:T(8,128)(2,1)S(1)} %get-tuple-element.71, bf16[256,36,188]{0,2,1:T(8,128)(2,1)S(1)} %get-tuple-element.72, bf16[256,36,188]{0,2,1:T(8,128)(2,1)S(1)} %fusion.32), kind=kLoop, calls=%fused_computation.19 | loop fusion | flops 27721728 | bytes 24256512 | tf_op jit(solution)/shard_map/stack | solution.py:31
  533.3 7.2 %fusion.4 = f32[256,36,2,128]{3,0,2,1:T(8,128)S(1)} fusion(bf16[256,36,1,376]{0,3,2,1:T(8,128)(2,1)} %get-tuple-element.74, bf16[256,36,1,376]{0,3,2,1:T(8,128)(2,1)} %get-tuple-element.73, bf16[376,128,1,1]{1,0,2,3:T(8,128)(2,1)S(1)} %reshape.67), kind=kOutput, calls=%fused_computation.15 | convolution fusion | flops 1781121024 | bytes 23394304 | tf_op jit(solution)/shard_map/dot_general | solution.py:32
  (254 shorter events, 226.4 us)
Async XLA Ops:
  15.1 8.6 %copy-start.6 = (s32[8]{0:T(128)S(1)}, s32[8]{0:T(128)}, u32[]{:S(2)}) copy-start(s32[8]{0:T(128)} %param.7) | copy-start | bytes 100
  15.1 8.8 %copy-start.4 = (bf16[2,188,128]{2,0,1:T(2,128)(2,1)S(1)}, bf16[2,188,128]{2,0,1:T(2,128)(2,1)}, u32[]{:S(2)}) copy-start(bf16[2,188,128]{2,0,1:T(2,128)(2,1)} %param.9) | copy-start | bytes 288772
  15.1 8.8 %copy-start.5 = (s32[36]{0:T(128)S(1)}, s32[36]{0:T(128)}, u32[]{:S(2)}) copy-start(s32[36]{0:T(128)} %param.8) | copy-start | bytes 436
  17.1 81.6 %all-to-all-start = ((bf16[16,16,8,376]{3,2,1,0:T(8,128)(2,1)}), bf16[16,16,8,376]{3,2,1,0:T(8,128)(2,1)S(1)}, u32[]{:S(2)}, u32[]{:S(2)}) async-start(bf16[16,16,8,376]{3,2,1,0:T(8,128)(2,1)} %reshape.61), calls=%async_computation | async-start | bytes 3145728 | tf_op jit(solution)/shard_map/all_to_all | solution.py:58
  23.5 477.5 %all-gather.2.cloned.1.call-start = ((), (), s32[]{:S(2)}) async-start(), calls=%async_computation.1 | async-start | bytes 7380992 | tf_op jit(solution)/shard_map/all_gather | solution.py:105
  107.1 5.4 copy-start.2
  123.2 5.4 copy-start.1
  123.2 5.4 copy-start.2
  139.3 5.4 copy-start.1
  139.3 5.4 copy-start.2
  155.4 5.4 copy-start.1
  155.4 5.4 copy-start.2
  171.5 5.4 copy-start.1
  171.5 5.4 copy-start.2
  187.6 5.4 copy-start.1
  187.6 5.4 copy-start.2
  203.6 5.4 copy-start.1
  203.6 5.4 copy-start.2
  219.7 5.4 copy-start.2
  235.8 5.4 copy-start.2
  251.9 5.4 copy-start.2
  268.0 5.4 copy-start.1
  268.0 5.4 copy-start.2
  284.1 5.4 copy-start.2
  300.1 5.4 copy-start.2
  316.2 5.4 copy-start.2
  332.3 5.4 copy-start.2
  348.4 5.4 copy-start.2
  364.5 5.4 copy-start.2
  380.6 5.4 copy-start.2
  396.7 5.4 copy-start.2
  412.7 5.4 copy-start.2
  (34 other events, 137.7 us)
Sparse Core Ops, SparseCore 0:
  431.8 69.0 all-gather.1
where the time goes:
time: 554 us; the launch traced here: 550 us
  matrix products  303 us (55%)
  blocking collectives  74 us (13%)
  waiting for transfers between devices  67.1 us (12%)
  other arithmetic  43.2 us (8%)
  local copies, waits for them, and re-layouts  40.7 us (7%)
  between operations  14.2 us (3%)
  starting transfers between devices  6.39 us (1%)
    dot_general x80, matrix products, apply_white(): return jnp.einsum('kij,kjb->kib', matrix, vector, precision=highest)  294 us
    psum x1, blocking collectives, on_device(): steering = lax.psum(steer_local, 'tm')  74 us
    all_gather x1, waiting for transfers between devices, on_device(): collected = lax.all_gather(flat_pair, 'tm', axis=0, tiled=True)  67.1 us
    mul x20, other arithmetic, power_turn(): return (image_real * factor[:, None, :], image_imag * factor[:, None, :])  25.8 us
    unnamed x11, local copies, waits for them, and re-layouts  11.5 us
  transfers between devices with their start and end apart: 2, of which 1 were waited for; matrix products, arithmetic and copies ran while one was open for 1% of the time, Pallas kernels for 0%

commit v1 on v0

v1 whole, which is shorter than its diff:
```python
import functools
import jax
import jax.numpy as jnp
from jax import lax
from jax.experimental import pallas as pl
from jax.experimental.pallas import tpu as pltpu
from jax.sharding import PartitionSpec as P

ITERS = 20
ROUGH = 0


def off_flags(moments, starts, range_len):
    inside = (moments[None, :] >= starts[:, None]) & (
        moments[None, :] < starts[:, None] + range_len
    )
    return jnp.any(inside, axis=0)


def split_two(value):
    high = value.astype(jnp.bfloat16)
    return high, (value - high.astype(jnp.float32)).astype(jnp.bfloat16)


def dot32(a, b):
    return jnp.dot(a, b, preferred_element_type=jnp.float32)


def power_kernel(volt_ref, mask_ref, count_ref, steer_ref, out_ref, real_hi, real_lo, imag_hi, imag_lo):
    senders, chans, rows_dev, ports = volt_ref.shape
    rows = senders * rows_dev
    beams = steer_ref.shape[0] // 2
    chunk = 256
    steer_real = steer_ref[:beams]
    steer_imag = steer_ref[beams:]
    gain = steer_real * steer_real + steer_imag * steer_imag
    row_id = lax.broadcasted_iota(jnp.int32, (chunk, chunk), 0)
    col_id = lax.broadcasted_iota(jnp.int32, (chunk, chunk), 1)
    even = lax.rem(row_id, 2) == 0
    turn = jnp.where(
        even & (col_id == row_id + 1), 1.0, jnp.where((~even) & (col_id == row_id - 1), -1.0, 0.0)
    ).astype(jnp.bfloat16)
    inverse_noise = []
    for c in range(chans):
        samples = volt_ref[:, c].reshape(rows, ports)
        mask = mask_ref[...]
        on_source = samples * mask
        wide = samples.astype(jnp.float32)
        off_power = jnp.sum(
            wide * wide * (1.0 - mask.astype(jnp.float32)), axis=0, keepdims=True
        )
        inverse_noise.append(1.0 / (off_power / count_ref[...] + 1e-06))
        turned = [
            dot32(turn, on_source[k : k + chunk]).astype(jnp.bfloat16)
            for k in range(0, rows, chunk)
        ]
        turned = turned[0] if len(turned) == 1 else jnp.concatenate(turned, axis=0)
        dims = (((0,), (0,)), ((), ()))
        corr_real = lax.dot_general(on_source, samples, dims, preferred_element_type=jnp.float32)
        corr_imag = lax.dot_general(turned, samples, dims, preferred_element_type=jnp.float32)
        real_hi[c], real_lo[c] = split_two(corr_real)
        imag_hi[c], imag_lo[c] = split_two(corr_imag)

    def mix(c, state, rough):
        if rough:
            high = state.astype(jnp.bfloat16)
            by_real = dot32(high, real_hi[c])
            by_imag = dot32(high, imag_hi[c])
        else:
            high, low = split_two(state)
            both = jnp.concatenate([high, low], axis=0)
            by_real = dot32(both, real_hi[c])
            by_imag = dot32(both, imag_hi[c])
            by_real = by_real[: 2 * beams] + by_real[2 * beams :] + dot32(high, real_lo[c])
            by_imag = by_imag[: 2 * beams] + by_imag[2 * beams :] + dot32(high, imag_lo[c])
        return by_real[:beams] + by_imag[beams:], by_real[beams:] - by_imag[:beams]

    weighting = [gain * inv for inv in inverse_noise]

    def power_turn(rough, counter, states):
        new_states = []
        for c in range(chans):
            mixed_real, mixed_imag = mix(c, states[c], rough)
            next_real = weighting[c] * mixed_real
            next_imag = weighting[c] * mixed_imag
            total = jnp.sum(
                next_real * mixed_real + next_imag * mixed_imag, axis=1, keepdims=True
            )
            factor = lax.rsqrt(total / (2 * ports) + 1e-06)
            new_states.append(jnp.concatenate([next_real * factor, next_imag * factor], axis=0))
        return tuple(new_states)

    states = tuple(
        jnp.concatenate([gain * jnp.sqrt(inv), jnp.zeros_like(gain)], axis=0)
        for inv in inverse_noise
    )
    if ROUGH > 0:
        states = lax.fori_loop(0, ROUGH, functools.partial(power_turn, True), states)
    states = lax.fori_loop(ROUGH, ITERS - 1, functools.partial(power_turn, False), states)
    for c in range(chans):
        mixed_real, mixed_imag = mix(c, states[c], False)
        total = jnp.sum(
            weighting[c] * mixed_real * mixed_real + weighting[c] * mixed_imag * mixed_imag,
            axis=1,
            keepdims=True,
        )
        factor = lax.rsqrt(total / (2 * ports) + 1e-06) * inverse_noise[c]
        weight_real = (steer_real * mixed_real - steer_imag * mixed_imag) * factor
        weight_imag = (steer_real * mixed_imag + steer_imag * mixed_real) * factor
        out_ref[c] = jnp.concatenate([weight_real, weight_imag], axis=0).astype(jnp.bfloat16)


def power_weights(arrived, mask, count, steering):
    senders, chans, rows_dev, ports = arrived.shape
    beams2 = steering.shape[0]
    work = chans * ITERS * 2 * ports * ports * 3 * beams2 * 2
    return pl.pallas_call(
        power_kernel,
        out_shape=jax.ShapeDtypeStruct((chans, beams2, ports), jnp.bfloat16),
        in_specs=[pl.BlockSpec(memory_space=pltpu.VMEM)] * 4,
        out_specs=pl.BlockSpec(memory_space=pltpu.VMEM),
        scratch_shapes=[pltpu.VMEM((chans, ports, ports), jnp.bfloat16)] * 4,
        compiler_params=pltpu.CompilerParams(vmem_limit_bytes=32 * 1024 * 1024),
        cost_estimate=pl.CostEstimate(
            flops=10 * work, bytes_accessed=2 * arrived.size, transcendentals=0
        ),
    )(arrived, mask, count, steering)


def map_kernel(beams, weights_ref, pattern_ref, *rest):
    out_ref = rest[-1]
    _, chans, beams2, ports = weights_ref.shape
    padded = beams2 // 2
    pixels = pattern_ref.shape[1] // 2
    flat = weights_ref[0].reshape(chans * beams2, ports)
    response = dot32(flat, pattern_ref[...]).reshape(chans, 2, padded, 2 * pixels)
    real = response[:, 0, :, :pixels] + response[:, 1, :, pixels:]
    imag = response[:, 0, :, pixels:] - response[:, 1, :, :pixels]
    out_ref[0] = (real * real + imag * imag)[:, :beams]


def beam_power(gathered, patterns, part, parts, beams, before):
    senders, chans, beams2, ports = gathered.shape
    pixels = patterns.shape[1] // 2
    in_specs = [
        pl.BlockSpec((1, chans, beams2, ports), lambda i: (i, 0, 0, 0)),
        pl.BlockSpec((ports, 2 * pixels), lambda i: (0, 0)),
    ]
    operands = [gathered, patterns]
    aliases = {}
    if before is not None:
        in_specs.append(pl.BlockSpec(memory_space=pl.ANY))
        operands.append(before)
        aliases = {2: 0}
    return pl.pallas_call(
        functools.partial(map_kernel, beams),
        grid=(senders,),
        out_shape=jax.ShapeDtypeStruct((senders, parts * chans, beams, pixels), jnp.float32),
        in_specs=in_specs,
        out_specs=pl.BlockSpec((1, chans, beams, pixels), lambda i: (i, part, 0, 0)),
        input_output_aliases=aliases,
        compiler_params=pltpu.CompilerParams(vmem_limit_bytes=32 * 1024 * 1024),
    )(*operands)


def on_device(voltages, off_starts, pointing, patterns):
    devices = lax.axis_size("tm")
    position = lax.axis_index("tm")
    channels, samples_dev, _, ports = voltages.shape
    beams = pointing.shape[0]
    padded = -(-beams // 8) * 8
    per_dev = channels // devices
    parts = 4 if per_dev % 4 == 0 else per_dev
    chans = per_dev // parts
    rows_dev = 2 * samples_dev
    total_time = samples_dev * devices
    off_span = max(4, total_time // 32)
    is_off = off_flags(jnp.arange(total_time, dtype=jnp.int32), off_starts, off_span)
    off_count = jnp.sum(is_off.astype(jnp.float32))
    count = jnp.broadcast_to(off_count, (1, ports))
    mask = jnp.broadcast_to(
        jnp.repeat(~is_off, 2)[:, None], (2 * total_time, ports)
    ).astype(jnp.bfloat16)
    pixels = patterns.shape[2]
    pixel_ids = position * pixels + jnp.arange(pixels, dtype=jnp.int32)
    wanted = jnp.pad(pointing, (0, padded - beams), constant_values=-1)
    selector = (wanted[:, None] == pixel_ids[None, :]).astype(jnp.bfloat16)
    picked = jnp.einsum("rpx,bx->rbp", patterns, selector, preferred_element_type=jnp.float32)
    picked = picked.astype(jnp.bfloat16).reshape(1, 2 * padded, ports)
    spread = jnp.broadcast_to(picked, (devices, 2 * padded, ports))
    spread = lax.all_to_all(spread, "tm", split_axis=0, concat_axis=0, tiled=True)
    steering = jnp.sum(spread.astype(jnp.float32), axis=0)
    blocks = voltages.reshape(devices, parts, chans, rows_dev, ports)
    pattern_rows = jnp.concatenate([patterns[0], patterns[1]], axis=1)
    arrived = [
        lax.all_to_all(blocks[:, k], "tm", split_axis=0, concat_axis=0, tiled=True)
        for k in range(parts)
    ]
    weights = [power_weights(a, mask, count, steering) for a in arrived]
    gathered = [lax.all_gather(w, "tm", axis=0) for w in weights]
    maps = None
    for k in range(parts):
        maps = beam_power(gathered[k], pattern_rows, k, parts, beams, maps)
    flat = jnp.stack(weights).reshape(per_dev, 2, padded, ports)[:, :, :beams]
    return (
        flat.reshape(per_dev, 2, beams * ports),
        maps.reshape(channels, beams, pixels),
    )


def solution(mesh):
    in_specs = (P(None, ("groups", "tm"), None, None), P("groups"), P(), P(None, None, "tm"))
    out_specs = (P(("groups", "tm"), None, None), P("groups", None, "tm"))
    return jax.shard_map(
        on_device, mesh=mesh, in_specs=in_specs, out_specs=out_specs, check_vma=False
    )
```

time: 554 us -> 272 us (0.49)
  matrix products: 303 us -> 1.08 us
  Pallas kernels: 0 us -> 61.5 us
  other arithmetic: 43.2 us -> 2.17 us
  starting transfers between devices: 6.39 us -> 12.8 us
    dot_general x83 -> x1, matrix products: 303 us -> 1.08 us  [on_device(): jnp.einsum('rpx,bx->rbp', patterns, selector, preferred_element_type=jnp....]
    psum x1 -> x0, blocking collectives: 74 us -> none  [on_device(): steering = lax.psum(steer_local, 'tm')]
    all_to_all x0 -> x3, blocking collectives: none -> 70.7 us  [on_device(): lax.all_to_all(blocks[:, k], 'tm', split_axis=0, concat_axis=0, tiled=True)]
    pallas_call x0 -> x8, Pallas kernels: none -> 61.5 us  [the longest x4 49 us: power_weights(): pl.pallas_call(power_kernel, out_shape=jax.ShapeDtypeStruct((chans, beams...]
    mul x22 -> x0, other arithmetic: 29.4 us -> none  [the longest x20 25.8 us: power_turn(): return (image_real * factor[:, None, :], image_imag * factor[:, None, :])]
    unnamed x11 -> x27, local copies, waits for them, and re-layouts: 11.5 us -> 32.3 us
    all_gather x1 -> x4, waiting for transfers between devices: 67.1 us -> 50.5 us  [on_device(): gathered = [lax.all_gather(w, 'tm', axis=0) for w in weights]]
    all_to_all x1 -> x2, waiting for transfers between devices: 0.01 us -> 13 us  [the longest x1 11.4 us: on_device(): lax.all_to_all(blocks[:, k], 'tm', split_axis=0, concat_axis=0, tiled=True)]
  transfers between devices with their start and end apart: 2 -> 6, of which waited for: 1 -> 4; matrix products, arithmetic and copies ran while one was open for 1% -> 7% of each run, Pallas kernels for 0% -> 17%
where the time goes in v1:
time: 272 us; the launch traced here: 268 us
  blocking collectives  70.7 us (26%)
  waiting for transfers between devices  63.5 us (23%)
  Pallas kernels  61.5 us (23%)
  local copies, waits for them, and re-layouts  42.3 us (16%)
  between operations  13.9 us (5%)
  starting transfers between devices  12.8 us (5%)
    all_to_all x3, blocking collectives, on_device(): lax.all_to_all(blocks[:, k], 'tm', split_axis=0, concat_axis=0, tiled=True)  70.7 us
    all_gather x4, waiting for transfers between devices, on_device(): gathered = [lax.all_gather(w, 'tm', axis=0) for w in weights]  50.5 us
    pallas_call x4, Pallas kernels, power_weights(): pl.pallas_call(power_kernel, out_shape=jax.ShapeDtypeStruct((chans, beams...  49 us
    unnamed x27, local copies, waits for them, and re-layouts  32.3 us
    pallas_call x4, Pallas kernels, beam_power(): pl.pallas_call(functools.partial(map_kernel, beams), grid=(senders,), out...  12.4 us
    all_to_all x1, waiting for transfers between devices, on_device(): lax.all_to_all(blocks[:, k], 'tm', split_axis=0, concat_axis=0, tiled=True)  11.4 us
    all_to_all x1, starting transfers between devices, on_device(): lax.all_to_all(spread, 'tm', split_axis=0, concat_axis=0, tiled=True)  6.36 us
    all_to_all x1, starting transfers between devices, on_device(): lax.all_to_all(blocks[:, k], 'tm', split_axis=0, concat_axis=0, tiled=True)  6.3 us
  transfers between devices with their start and end apart: 6, of which 4 were waited for; matrix products, arithmetic and copies ran while one was open for 7% of the time, Pallas kernels for 17%

profile of v1, /device:TPU:29, one launch (start us, length us, event | category | flops | bytes accessed | tf_op | source)
XLA Modules:
  0.0 267.9 jit_solution(13495480927493131624)
XLA Ops:
  9.8 6.4 %all-to-all-start.1 = ((bf16[16,80,188]{2,1,0:T(8,128)(2,1)}), bf16[16,80,188]{2,1,0:T(8,128)(2,1)S(1)}, u32[]{:S(2)}, u32[]{:S(2)}) async-start(bf16[16,80,188]{2,1,0:T(8,128)(2,1)} %broadcast_in_dim.28), calls=%async_computation.1 | async-start | bytes 1310720 | tf_op jit(solution)/shard_map/all_to_all | solution.py:191
  16.2 7.9 %copy.35 = bf16[256,8,2,188]{3,2,1,0:T(2,128)(2,1)S(1)} copy(bf16[256,8,2,188]{0,2,3,1:T(2,128)(2,1)} %param.4) | data formatting | bytes 3080192 | tf_op args[0]
  24.1 3.1 %reshape.28 = bf16[16,4,4,16,188]{4,3,2,1,0:T(8,128)(2,1)} reshape(bf16[256,8,2,188]{3,2,1,0:T(2,128)(2,1)S(1)} %copy.35) | data formatting | bytes 3080192 | tf_op jit(solution)/shard_map/reshape | solution.py:193
  27.2 2.5 slice_bitcast_fusion.3
  29.7 1.6 all-to-all-done.1
  31.3 6.3 %all-to-all-start = ((bf16[16,4,16,188]{3,2,1,0:T(8,128)(2,1)}), bf16[16,4,16,188]{3,2,1,0:T(8,128)(2,1)S(1)}, u32[]{:S(2)}, u32[]{:S(2)}) async-start(bf16[16,4,16,188]{3,2,1,0:T(8,128)(2,1)} %get-tuple-element.10), calls=%async_computation | async-start | bytes 1048576 | tf_op jit(solution)/shard_map/all_to_all | solution.py:196
  38.7 11.4 %all-to-all-done.volt_ref = bf16[16,4,16,188]{3,2,1,0:T(8,128)(2,1)S(1)} async-done(((bf16[16,4,16,188]{3,2,1,0:T(8,128)(2,1)}), bf16[16,4,16,188]{3,2,1,0:T(8,128)(2,1)S(1)}, u32[]{:S(2)}, u32[]{:S(2)}) %all-to-all-start) | async-done | bytes 385056 | tf_op jit(solution)/shard_map/all_to_all | solution.py:196
  50.9 12.3 %shard_map.59 = bf16[4,80,188]{2,1,0:T(8,128)(2,1)} custom-call(bf16[16,4,16,188]{3,2,1,0:T(8,128)(2,1)S(1)} %all-to-all-done.volt_ref, bf16[256,188]{1,0:T(8,128)(2,1)S(1)} %broadcast_in_dim.11.mask_ref, f32[1,188]{1,0:T(1,128)S(1)} %broadcast_in_dim.12.count_ref, f32[80,188]{1,0:T(8,128)S(1)} %convert_reduce_fusion.steer_ref), custom_call_target="tpu_custom_call" | custom-call | flops 27144192000 | bytes 385024 | tf_op jit(solution)/shard_map/pallas_call | solution.py:117
  63.2 23.5 %all_to_all.25.volt_ref = bf16[16,4,16,188]{3,2,1,0:T(8,128)(2,1)S(1)} all-to-all(bf16[16,4,16,188]{3,2,1,0:T(8,128)(2,1)S(1)} %get-tuple-element.12), channel_id=1, replica_groups=mesh['groups'=2,'tm'=16] {'tm'}, dimensions={0} | all-to-all | bytes 770048 | tf_op jit(solution)/shard_map/all_to_all | solution.py:196
  86.7 12.2 %shard_map.60 = bf16[4,80,188]{2,1,0:T(8,128)(2,1)} custom-call(bf16[16,4,16,188]{3,2,1,0:T(8,128)(2,1)S(1)} %all_to_all.25.volt_ref, bf16[256,188]{1,0:T(8,128)(2,1)S(1)} %broadcast_in_dim.11.mask_ref, f32[1,188]{1,0:T(1,128)S(1)} %broadcast_in_dim.12.count_ref, f32[80,188]{1,0:T(8,128)S(1)} %convert_reduce_fusion.steer_ref), custom_call_target="tpu_custom_call" | custom-call | flops 27144192000 | bytes 385024 | tf_op jit(solution)/shard_map/pallas_call | solution.py:117
  99.0 18.6 %all_to_all.26.volt_ref = bf16[16,4,16,188]{3,2,1,0:T(8,128)(2,1)S(1)} all-to-all(bf16[16,4,16,188]{3,2,1,0:T(8,128)(2,1)S(1)} %get-tuple-element.11), channel_id=1, replica_groups=mesh['groups'=2,'tm'=16] {'tm'}, dimensions={0} | all-to-all | bytes 770048 | tf_op jit(solution)/shard_map/all_to_all | solution.py:196
  117.6 12.2 %shard_map.61 = bf16[4,80,188]{2,1,0:T(8,128)(2,1)} custom-call(bf16[16,4,16,188]{3,2,1,0:T(8,128)(2,1)S(1)} %all_to_all.26.volt_ref, bf16[256,188]{1,0:T(8,128)(2,1)S(1)} %broadcast_in_dim.11.mask_ref, f32[1,188]{1,0:T(1,128)S(1)} %broadcast_in_dim.12.count_ref, f32[80,188]{1,0:T(8,128)S(1)} %convert_reduce_fusion.steer_ref), custom_call_target="tpu_custom_call" | custom-call | flops 27144192000 | bytes 385024 | tf_op jit(solution)/shard_map/pallas_call | solution.py:117
  129.9 28.6 %all_to_all.27.volt_ref = bf16[16,4,16,188]{3,2,1,0:T(8,128)(2,1)S(1)} all-to-all(bf16[16,4,16,188]{3,2,1,0:T(8,128)(2,1)S(1)} %get-tuple-element.13), channel_id=1, replica_groups=mesh['groups'=2,'tm'=16] {'tm'}, dimensions={0} | all-to-all | bytes 770048 | tf_op jit(solution)/shard_map/all_to_all | solution.py:196
  158.6 12.3 %shard_map.62 = bf16[4,80,188]{2,1,0:T(8,128)(2,1)} custom-call(bf16[16,4,16,188]{3,2,1,0:T(8,128)(2,1)S(1)} %all_to_all.27.volt_ref, bf16[256,188]{1,0:T(8,128)(2,1)S(1)} %broadcast_in_dim.11.mask_ref, f32[1,188]{1,0:T(1,128)S(1)} %broadcast_in_dim.12.count_ref, f32[80,188]{1,0:T(8,128)S(1)} %convert_reduce_fusion.steer_ref), custom_call_target="tpu_custom_call" | custom-call | flops 27144192000 | bytes 385024 | tf_op jit(solution)/shard_map/pallas_call | solution.py:117
  172.2 1.8 reshape.37
  174.0 1.7 copy-done.6
  175.8 3.1 %shard_map.63.rest_0_ = f32[16,16,36,128]{3,2,1,0:T(8,128)S(1)} custom-call(bf16[16,4,80,188]{3,2,1,0:T(8,128)(2,1)S(1)} %bitcast.38, bf16[188,256]{1,0:T(8,128)(2,1)S(1)} %pad_maximum_fusion.1.pattern_ref), custom_call_target="tpu_custom_call" | custom-call | tf_op jit(solution)/shard_map/pallas_call | solution.py:155
  178.9 2.3 copy-done
  181.2 2.5 copy-done.1
  183.7 1.7 copy-done.7
  185.4 3.1 %shard_map.64.rest_0_ = f32[16,16,36,128]{3,2,1,0:T(8,128)S(1)} custom-call(bf16[16,4,80,188]{3,2,1,0:T(8,128)(2,1)S(1)} %bitcast.39, bf16[188,256]{1,0:T(8,128)(2,1)S(1)} %pad_maximum_fusion.1.pattern_ref, f32[16,16,36,128]{3,2,1,0:T(8,128)S(1)} %copy-done.1), custom_call_target="tpu_custom_call", output_to_operand_aliasing={{}: (2, {})} | custom-call | tf_op jit(solution)/shard_map/pallas_call | solution.py:155
  188.6 2.3 copy-done.2
  190.9 15.5 %all-gather.11.cloned.1.call-done = bf16[64,80,188]{2,1,0:T(8,128)(2,1)} async-done(((bf16[4,80,188]{2,1,0:T(8,128)(2,1)}), bf16[64,80,188]{2,1,0:T(8,128)(2,1)}) %all-gather.11.cloned.1.call-update) | async-done | bytes 1925136 | tf_op jit(solution)/shard_map/all_gather | solution.py:200
  206.4 2.5 copy-done.3
  208.9 1.7 copy-done.8
  210.6 3.1 %shard_map.65.rest_0_ = f32[16,16,36,128]{3,2,1,0:T(8,128)S(1)} custom-call(bf16[16,4,80,188]{3,2,1,0:T(8,128)(2,1)S(1)} %bitcast.40, bf16[188,256]{1,0:T(8,128)(2,1)S(1)} %pad_maximum_fusion.1.pattern_ref, f32[16,16,36,128]{3,2,1,0:T(8,128)S(1)} %copy-done.3), custom_call_target="tpu_custom_call", output_to_operand_aliasing={{}: (2, {})} | custom-call | tf_op jit(solution)/shard_map/pallas_call | solution.py:155
  213.7 2.3 copy-done.4
  216.0 35.0 %all-gather.9.cloned.1.call-done = bf16[64,80,188]{2,1,0:T(8,128)(2,1)} async-done(((bf16[4,80,188]{2,1,0:T(8,128)(2,1)}), bf16[64,80,188]{2,1,0:T(8,128)(2,1)}) %all-gather.9.cloned.1.call-update) | async-done | bytes 1925136 | tf_op jit(solution)/shard_map/all_gather | solution.py:200
  251.0 2.5 copy-done.5
  253.5 1.7 copy-done.9
  255.2 3.1 %shard_map.66 = f32[16,16,36,128]{3,2,1,0:T(8,128)S(1)} custom-call(bf16[16,4,80,188]{3,2,1,0:T(8,128)(2,1)S(1)} %bitcast.41, bf16[188,256]{1,0:T(8,128)(2,1)S(1)} %pad_maximum_fusion.1.pattern_ref, f32[16,16,36,128]{3,2,1,0:T(8,128)S(1)} %copy-done.5), custom_call_target="tpu_custom_call", output_to_operand_aliasing={{}: (2, {})} | custom-call | tf_op jit(solution)/shard_map/pallas_call | solution.py:155
  258.3 3.0 %copy.45 = f32[256,36,128]{2,0,1:T(8,128)} copy(f32[256,36,128]{2,1,0:T(8,128)S(1)} %bitcast.37) | data formatting | bytes 9437184
  (41 shorter events, 6.1 us)
Async XLA Ops:
  9.8 21.4 %all-to-all-start.1 = ((bf16[16,80,188]{2,1,0:T(8,128)(2,1)}), bf16[16,80,188]{2,1,0:T(8,128)(2,1)S(1)}, u32[]{:S(2)}, u32[]{:S(2)}) async-start(bf16[16,80,188]{2,1,0:T(8,128)(2,1)} %broadcast_in_dim.28), calls=%async_computation.1 | async-start | bytes 1310720 | tf_op jit(solution)/shard_map/all_to_all | solution.py:191
  27.2 10.4 %copy-start.11 = (s32[8]{0:T(128)S(1)}, s32[8]{0:T(128)}, u32[]{:S(2)}) copy-start(s32[8]{0:T(128)} %param.5) | copy-start | bytes 100
  31.3 18.8 %all-to-all-start = ((bf16[16,4,16,188]{3,2,1,0:T(8,128)(2,1)}), bf16[16,4,16,188]{3,2,1,0:T(8,128)(2,1)S(1)}, u32[]{:S(2)}, u32[]{:S(2)}) async-start(bf16[16,4,16,188]{3,2,1,0:T(8,128)(2,1)} %get-tuple-element.10), calls=%async_computation | async-start | bytes 1048576 | tf_op jit(solution)/shard_map/all_to_all | solution.py:196
  37.6 136.5 %all-gather.15.cloned.1.call-start = ((), (), s32[]{:S(2)}) async-start(), calls=%async_computation.8 | async-start | bytes 2785280 | tf_op jit(solution)/shard_map/all_gather | solution.py:200
  63.2 118.1 %all-gather.13.cloned.1.call-start = ((), (), s32[]{:S(2)}) async-start(), calls=%async_computation.7 | async-start | bytes 2785280 | tf_op jit(solution)/shard_map/all_gather | solution.py:200
  99.0 107.4 %all-gather.11.cloned.1.call-start = ((), (), s32[]{:S(2)}) async-start(), calls=%async_computation.6 | async-start | bytes 2785280 | tf_op jit(solution)/shard_map/all_gather | solution.py:200
  129.9 121.1 %all-gather.9.cloned.1.call-start = ((), (), s32[]{:S(2)}) async-start(), calls=%async_computation.5 | async-start | bytes 2785280 | tf_op jit(solution)/shard_map/all_gather | solution.py:200
  158.6 12.3 %copy-start.10 = (bf16[2,188,128]{2,0,1:T(2,128)(2,1)S(1)}, bf16[2,188,128]{2,0,1:T(2,128)(2,1)}, u32[]{:S(2)}) copy-start(bf16[2,188,128]{2,0,1:T(2,128)(2,1)} %param.7) | copy-start | bytes 288772
  174.0 1.7 copy-start.6
  178.9 2.3 copy-start
  181.2 2.5 copy-start.1
  183.7 1.7 copy-start.7
  188.6 2.3 copy-start.2
  206.4 2.5 copy-start.3
  208.9 1.7 copy-start.8
  213.7 2.3 copy-start.4
  251.0 2.5 copy-start.5
  253.5 1.7 copy-start.9
Sparse Core Ops, SparseCore 0:
  63.3 46.4 all-gather.14
  112.1 49.1 all-gather.12
  163.6 42.7 all-gather.10
  209.1 41.8 all-gather.8

commit v2 on v1

v2 whole, which is shorter than its diff:
```python
import functools
import jax
import jax.numpy as jnp
from jax import lax
from jax.experimental import pallas as pl
from jax.experimental.pallas import tpu as pltpu
from jax.sharding import PartitionSpec as P

ITERS = 20
MESH = pl.DeviceIdType.MESH


def off_flags(moments, starts, range_len):
    inside = (moments[None, :] >= starts[:, None]) & (
        moments[None, :] < starts[:, None] + range_len
    )
    return jnp.any(inside, axis=0)


def split_two(value):
    high = value.astype(jnp.bfloat16)
    return high, (value - high.astype(jnp.float32)).astype(jnp.bfloat16)


def dot32(a, b):
    return jnp.dot(a, b, preferred_element_type=jnp.float32)


def correlate(volt_ref, part, c, mask, count):
    senders, rows_dev, width = volt_ref.shape[1:]
    ports = width // 2
    samples_dev = mask.shape[0] // senders
    wide = volt_ref[part].astype(jnp.float32)
    wide = wide[:, c * samples_dev : (c + 1) * samples_dev].reshape(senders * samples_dev, width)
    first, second = wide[:, :ports], wide[:, ports:]
    on_first, on_second = first * mask, second * mask
    power = (first * first + second * second) * (1.0 - mask)
    noise_power = jnp.sum(power, axis=0, keepdims=True) / count + 1e-06
    pair = jnp.concatenate([first, second], axis=0).astype(jnp.bfloat16)
    on_pair = jnp.concatenate([on_first, on_second], axis=0).astype(jnp.bfloat16)
    turned = jnp.concatenate([on_second, -on_first], axis=0).astype(jnp.bfloat16)
    dims = (((0,), (0,)), ((), ()))
    corr_real = lax.dot_general(on_pair, pair, dims, preferred_element_type=jnp.float32)
    corr_imag = lax.dot_general(turned, pair, dims, preferred_element_type=jnp.float32)
    return corr_real, corr_imag, 1.0 / noise_power


def compute_part(part, volt_ref, mask_ref, count_ref, steer_ref, out_ref, mats):
    real_hi, real_lo, imag_hi, imag_lo = mats
    chans = real_hi.shape[0]
    ports = real_hi.shape[1]
    beams = steer_ref.shape[0] // 2
    steer_real = steer_ref[:beams]
    steer_imag = steer_ref[beams:]
    gain = steer_real * steer_real + steer_imag * steer_imag
    inverse_noise = []
    for c in range(chans):
        corr_real, corr_imag, inverse = correlate(
            volt_ref, part, c, mask_ref[...], count_ref[...]
        )
        inverse_noise.append(inverse)
        real_hi[c], real_lo[c] = split_two(corr_real)
        imag_hi[c], imag_lo[c] = split_two(corr_imag)

    def mix(c, state):
        high, low = split_two(state)
        both = jnp.concatenate([high, low], axis=0)
        by_real = dot32(both, real_hi[c])
        by_imag = dot32(both, imag_hi[c])
        by_real = by_real[: 2 * beams] + by_real[2 * beams :] + dot32(high, real_lo[c])
        by_imag = by_imag[: 2 * beams] + by_imag[2 * beams :] + dot32(high, imag_lo[c])
        return by_real[:beams] + by_imag[beams:], by_real[beams:] - by_imag[:beams]

    weighting = [gain * inv for inv in inverse_noise]

    def power_turn(counter, states):
        new_states = []
        for c in range(chans):
            mixed_real, mixed_imag = mix(c, states[c])
            next_real = weighting[c] * mixed_real
            next_imag = weighting[c] * mixed_imag
            total = jnp.sum(
                next_real * mixed_real + next_imag * mixed_imag, axis=1, keepdims=True
            )
            factor = lax.rsqrt(total / (2 * ports) + 1e-06)
            new_states.append(jnp.concatenate([next_real * factor, next_imag * factor], axis=0))
        return tuple(new_states)

    states = tuple(
        jnp.concatenate([gain * jnp.sqrt(inv), jnp.zeros_like(gain)], axis=0)
        for inv in inverse_noise
    )
    states = lax.fori_loop(0, ITERS - 1, power_turn, states)
    results = []
    for c in range(chans):
        mixed_real, mixed_imag = mix(c, states[c])
        total = jnp.sum(
            weighting[c] * mixed_real * mixed_real + weighting[c] * mixed_imag * mixed_imag,
            axis=1,
            keepdims=True,
        )
        factor = lax.rsqrt(total / (2 * ports) + 1e-06) * inverse_noise[c]
        weight_real = (steer_real * mixed_real - steer_imag * mixed_imag) * factor
        weight_imag = (steer_real * mixed_imag + steer_imag * mixed_real) * factor
        results.append(jnp.concatenate([weight_real, weight_imag], axis=1))
    out_ref[part] = jnp.concatenate(results, axis=0).astype(jnp.bfloat16)


def exchange_kernel(
    dims, blocks_ref, pick_ref, mask_ref, count_ref, gathered_ref, own_ref,
    arrived, slots, partial, steer, real_hi, real_lo, imag_hi, imag_lo,
    volt_send, volt_recv, steer_send, steer_recv,
    z_send, z_recv, x_send, x_recv, core_send, core_recv, place_sem,
):
    depth, width, cores = dims
    devices = depth * width * cores
    parts = arrived.shape[0]
    me = lax.axis_index("tm")
    my_core = lax.rem(me, cores)
    my_x = lax.rem(me // cores, width)
    my_z = me // (cores * width)

    def device(z, x, core):
        return {"tm": (z * width + x) * cores + core}

    def remote(src, dst, send, recv, target):
        return pltpu.make_async_remote_copy(
            src_ref=src, dst_ref=dst, send_sem=send, recv_sem=recv,
            device_id=target, device_id_type=MESH,
        )

    def take(ref, sem):
        pltpu.make_async_copy(ref, ref, sem).wait()

    barrier = pltpu.get_barrier_semaphore()

    @pl.loop(1, devices)
    def _(step):
        pl.semaphore_signal(
            barrier, inc=1, device_id={"tm": lax.rem(me + step, devices)}, device_id_type=MESH
        )

    pl.semaphore_wait(barrier, devices - 1)

    def start_volts(part):
        @pl.loop(1, devices)
        def _(step):
            target = lax.rem(me + step, devices)
            remote(
                blocks_ref.at[target, part], arrived.at[part, me],
                volt_send.at[part], volt_recv.at[part], {"tm": target},
            ).start()

        pltpu.make_async_copy(
            blocks_ref.at[me, part], arrived.at[part, me], volt_recv.at[part]
        ).start()

    stages = (
        (cores, lambda d: device(my_z, my_x, lax.rem(my_core + d, cores))),
        (width, lambda d: device(my_z, lax.rem(my_x + d, width), my_core)),
        (depth, lambda d: device(lax.rem(my_z + d, depth), my_x, my_core)),
    )
    total = pick_ref[...].astype(jnp.float32)
    base = 0
    for number, (extent, target) in enumerate(stages):
        if extent == 1:
            continue
        partial[number] = total.astype(jnp.bfloat16)
        copies = [
            remote(
                partial.at[number], slots.at[base + d - 1],
                steer_send.at[base + d - 1], steer_recv.at[base + d - 1], target(d),
            )
            for d in range(1, extent)
        ]
        for copy in copies:
            copy.start()
        if number == 0:
            start_volts(0)
        for copy in copies:
            copy.wait()
        for d in range(1, extent):
            total = total + slots[base + d - 1].astype(jnp.float32)
        base += extent - 1
    steer[...] = total

    def z_row(part):
        return gathered_ref.at[part, my_core, my_x]

    def start_z(part):
        for d in range(1, depth):
            remote(
                own_ref.at[part], gathered_ref.at[part, my_core, my_x, my_z],
                z_send.at[part], z_recv.at[part], device(lax.rem(my_z + d, depth), my_x, my_core),
            ).start()
        pltpu.make_async_copy(
            own_ref.at[part], gathered_ref.at[part, my_core, my_x, my_z], place_sem.at[part]
        ).start()

    def start_x(part):
        take(own_ref.at[part], place_sem.at[part])
        take(gathered_ref.at[part, my_core, my_x, pl.ds(0, depth - 1)], z_recv.at[part])
        for d in range(1, width):
            remote(
                z_row(part), z_row(part), x_send.at[part], x_recv.at[part],
                device(my_z, lax.rem(my_x + d, width), my_core),
            ).start()

    def start_core(part):
        take(gathered_ref.at[part, my_core, pl.ds(0, width - 1)], x_recv.at[part])
        for d in range(1, cores):
            remote(
                gathered_ref.at[part, my_core], gathered_ref.at[part, my_core],
                core_send.at[part], core_recv.at[part],
                device(my_z, my_x, lax.rem(my_core + d, cores)),
            ).start()

    @pl.loop(0, parts)
    def _(part):
        take(arrived.at[part], volt_recv.at[part])

        @pl.when(part + 1 < parts)
        def _():
            start_volts(part + 1)

        compute_part(
            part, arrived, mask_ref, count_ref, steer, own_ref,
            (real_hi, real_lo, imag_hi, imag_lo),
        )
        start_z(part)

        @pl.when(part >= 1)
        def _():
            start_x(part - 1)

        @pl.when(part >= 2)
        def _():
            start_core(part - 2)

    if parts >= 2:
        start_core(parts - 2)
    start_x(parts - 1)
    start_core(parts - 1)

    @pl.loop(0, parts)
    def _(part):
        take(gathered_ref.at[part, pl.ds(0, cores - 1)], core_recv.at[part])
        take(arrived.at[part, pl.ds(0, devices - 1)], volt_send.at[part])
        take(gathered_ref.at[part, my_core, my_x, pl.ds(0, depth - 1)], z_send.at[part])
        take(gathered_ref.at[part, my_core, pl.ds(0, width - 1)], x_send.at[part])
        take(gathered_ref.at[part, pl.ds(0, cores - 1)], core_send.at[part])


def exchange(dims, chans, blocks, pick, mask, count):
    depth, width, cores = dims
    devices, parts, rows_dev, double = blocks.shape
    ports = double // 2
    beams2 = pick.shape[0]
    rows = chans * beams2 // 2
    hops = depth + width + cores - 3
    bf16, dma = jnp.bfloat16, pltpu.SemaphoreType.DMA
    vmem = pl.BlockSpec(memory_space=pltpu.VMEM)
    anywhere = pl.BlockSpec(memory_space=pl.ANY)
    return pl.pallas_call(
        functools.partial(exchange_kernel, dims),
        out_shape=(
            jax.ShapeDtypeStruct((parts, cores, width, depth, rows, double), bf16),
            jax.ShapeDtypeStruct((parts, rows, double), bf16),
        ),
        in_specs=[anywhere, vmem, vmem, vmem],
        out_specs=(anywhere, vmem),
        scratch_shapes=[
            pltpu.VMEM((parts, devices, rows_dev, double), bf16),
            pltpu.VMEM((hops, beams2, ports), bf16),
            pltpu.VMEM((3, beams2, ports), bf16),
            pltpu.VMEM((beams2, ports), jnp.float32),
        ]
        + [pltpu.VMEM((chans, ports, ports), bf16)] * 4
        + [dma((parts,)), dma((parts,)), dma((hops,)), dma((hops,))]
        + [dma((parts,))] * 7,
        compiler_params=pltpu.CompilerParams(
            collective_id=0, has_side_effects=True, vmem_limit_bytes=40 * 1024 * 1024
        ),
    )(blocks, pick, mask, count)


def map_kernel(beams, weights_ref, pattern_ref, out_ref):
    parts, _, _, _, rows, double = weights_ref.shape
    chans = out_ref.shape[1] // parts
    pixels = pattern_ref.shape[1] // 2
    flat = weights_ref[:, 0, 0, 0].reshape(parts * rows, double)
    response = dot32(flat, pattern_ref[...])
    real, imag = response[:, :pixels], response[:, pixels:]
    power = (real * real + imag * imag).reshape(parts * chans, rows // chans, pixels)
    out_ref[0] = power[:, :beams]


def beam_power(dims, chans, gathered, patterns, beams):
    depth, width, cores = dims
    parts, _, _, _, rows, double = gathered.shape
    pixels = patterns.shape[1] // 2
    senders = depth * width * cores
    return pl.pallas_call(
        functools.partial(map_kernel, beams),
        grid=(senders,),
        out_shape=jax.ShapeDtypeStruct((senders, parts * chans, beams, pixels), jnp.float32),
        in_specs=[
            pl.BlockSpec(
                (parts, 1, 1, 1, rows, double),
                lambda i: (0, i % cores, (i // cores) % width, i // (cores * width), 0, 0),
            ),
            pl.BlockSpec((double, 2 * pixels), lambda i: (0, 0)),
        ],
        out_specs=pl.BlockSpec((1, parts * chans, beams, pixels), lambda i: (i, 0, 0, 0)),
        compiler_params=pltpu.CompilerParams(vmem_limit_bytes=32 * 1024 * 1024),
    )(gathered, patterns)


def torus_dims(devices):
    cores = 2 if devices % 2 == 0 else 1
    chips = devices // cores
    width = 1
    while chips % (4 * width * width) == 0:
        width *= 2
    return chips // width, width, cores


def on_device(voltages, off_starts, pointing, patterns):
    devices = lax.axis_size("tm")
    position = lax.axis_index("tm")
    channels, samples_dev, _, ports = voltages.shape
    beams = pointing.shape[0]
    padded = -(-beams // 8) * 8
    per_dev = channels // devices
    parts = 4 if per_dev % 4 == 0 else 1
    chans = per_dev // parts
    dims = torus_dims(devices)
    total_time = samples_dev * devices
    off_span = max(4, total_time // 32)
    is_off = off_flags(jnp.arange(total_time, dtype=jnp.int32), off_starts, off_span)
    off_count = jnp.sum(is_off.astype(jnp.float32))
    count = jnp.broadcast_to(off_count, (1, ports))
    mask = jnp.broadcast_to((~is_off)[:, None], (total_time, ports)).astype(jnp.float32)
    pixels = patterns.shape[2]
    pixel_ids = position * pixels + jnp.arange(pixels, dtype=jnp.int32)
    wanted = jnp.pad(pointing, (0, padded - beams), constant_values=-1)
    selector = (wanted[:, None] == pixel_ids[None, :]).astype(jnp.bfloat16)
    picked = jnp.einsum("rpx,bx->rbp", patterns, selector, preferred_element_type=jnp.float32)
    picked = picked.astype(jnp.bfloat16).reshape(2 * padded, ports)
    blocks = voltages.reshape(devices, parts, chans * samples_dev, 2 * ports)
    pattern_rows = jnp.concatenate(
        [
            jnp.concatenate([patterns[0], patterns[1]], axis=1),
            jnp.concatenate([patterns[1], -patterns[0]], axis=1),
        ],
        axis=0,
    )
    gathered, own = exchange(dims, chans, blocks, picked, mask, count)
    maps = beam_power(dims, chans, gathered, pattern_rows, beams)
    own = own.reshape(per_dev, padded, 2, ports)[:, :beams].transpose(0, 2, 1, 3)
    return (
        own.reshape(per_dev, 2, beams * ports),
        maps.reshape(channels, beams, pixels),
    )


def solution(mesh):
    in_specs = (P(None, ("groups", "tm"), None, None), P("groups"), P(), P(None, None, "tm"))
    out_specs = (P(("groups", "tm"), None, None), P("groups", None, "tm"))
    return jax.shard_map(
        on_device, mesh=mesh, in_specs=in_specs, out_specs=out_specs, check_vma=False
    )
```

time: 272 us -> 149 us (0.55); the launches traced: 268 us -> 148 us
  blocking collectives: 70.7 us -> 0 us
  waiting for transfers between devices: 63.5 us -> 0 us
  Pallas kernels: 61.5 us -> 117 us
  local copies, waits for them, and re-layouts: 42.3 us -> 27.2 us
  between operations: 13.9 us -> 0.74 us
  starting transfers between devices: 12.8 us -> 0 us
    all_to_all x3 -> x0, blocking collectives: 70.7 us -> none  [on_device(): lax.all_to_all(blocks[:, k], 'tm', split_axis=0, concat_axis=0, tiled=True)]
    pallas_call x4 -> x1, Pallas kernels: 49 us -> 110 us  [exchange(): pl.pallas_call(functools.partial(exchange_kernel, dims), out_shape=(jax.S...]
    all_gather x4 -> x0, waiting for transfers between devices: 50.5 us -> none  [on_device(): gathered = [lax.all_gather(w, 'tm', axis=0) for w in weights]]
    all_to_all x2 -> x0, waiting for transfers between devices: 13 us -> none  [the longest x1 11.4 us: on_device(): lax.all_to_all(blocks[:, k], 'tm', split_axis=0, concat_axis=0, tiled=True)]
    all_to_all x2 -> x0, starting transfers between devices: 12.7 us -> none  [the longest x1 6.36 us: on_device(): lax.all_to_all(spread, 'tm', split_axis=0, concat_axis=0, tiled=True)]
    unnamed x27 -> x9, local copies, waits for them, and re-layouts: 32.3 us -> 19.8 us
    pallas_call x4 -> x1, Pallas kernels: 12.4 us -> 6.56 us  [beam_power(): pl.pallas_call(functools.partial(map_kernel, beams), grid=(senders,), out...]
    reshape x2 -> x3, local copies, waits for them, and re-layouts: 4.88 us -> 5.66 us  [the longest x1 4.86 us: on_device(): blocks = voltages.reshape(devices, parts, chans * samples_dev, 2 * ports)]
  transfers between devices with their start and end apart: 6 -> 0, of which waited for: 4 -> 0; matrix products, arithmetic and copies ran while one was open for 7% -> 0% of each run, Pallas kernels for 17% -> 0%
where the time goes in v2:
time: 149 us; the launch traced here: 148 us
  Pallas kernels  117 us (79%)
  local copies, waits for them, and re-layouts  27.2 us (18%)
  other arithmetic  2.06 us (1%)
    pallas_call x1, Pallas kernels, exchange(): pl.pallas_call(functools.partial(exchange_kernel, dims), out_shape=(jax.S...  110 us
    unnamed x9, local copies, waits for them, and re-layouts  19.8 us
    pallas_call x1, Pallas kernels, beam_power(): pl.pallas_call(functools.partial(map_kernel, beams), grid=(senders,), out...  6.56 us
    reshape x1, local copies, waits for them, and re-layouts, on_device(): blocks = voltages.reshape(devices, parts, chans * samples_dev, 2 * ports)  4.86 us

profile of v2, /device:TPU:29, one launch (start us, length us, event | category | flops | bytes accessed | tf_op | source)
XLA Modules:
  0.0 147.7 jit_solution(9578338578242382098)
XLA Ops:
  0.6 0.7 pad.4
  1.3 0.7 broadcast_add_fusion
  2.0 0.7 fusion.5
  2.7 0.6 convert_reduce_fusion
  3.3 0.6 broadcast_in_dim.5.count_ref
  4.0 1.1 convolution_convert_fusion
  5.0 0.9 copy.20
  6.0 0.1 broadcast_in_dim.4.mask_ref
  6.1 8.3 %copy.19 = bf16[256,8,2,188]{3,2,1,0:T(2,128)(2,1)} copy(bf16[256,8,2,188]{0,2,3,1:T(2,128)(2,1)} %param.4) | data formatting | bytes 3080192 | tf_op args[0]
  14.5 4.9 %reshape.30.blocks_ref = bf16[16,4,32,376]{3,2,1,0:T(8,128)(2,1)S(1)} reshape(bf16[256,8,2,188]{3,2,1,0:T(2,128)(2,1)} %copy.19) | data formatting | bytes 3080192 | tf_op jit(solution)/shard_map/reshape | solution.py:350
  19.3 110.0 %shard_map.59 = (bf16[4,2,2,4,160,376]{5,4,3,2,1,0:T(8,128)(2,1)S(1)}, bf16[4,160,376]{2,1,0:T(8,128)(2,1)S(1)}) custom-call(bf16[16,4,32,376]{3,2,1,0:T(8,128)(2,1)S(1)} %reshape.30.blocks_ref, bf16[80,188]{1,0:T(8,128)(2,1)S(1)} %bitcast.19, f32[128,188]{1,0:T(8,128)S(1)} %broadcast_in_dim.4.mask_ref, f32[1,188]{1,0:T(1,128)S(1)} %broadcast_in_dim.5.count_ref), custom_call_target="tpu_custom_call" | custom-call | tf_op jit(solution)/shard_map/pallas_call | solution.py:264
  129.3 0.0 copy-start
  129.3 3.1 %copy-done = bf16[4,2,2,4,160,376]{5,4,3,2,1,0:T(8,128)(2,1)} copy-done((bf16[4,2,2,4,160,376]{5,4,3,2,1,0:T(8,128)(2,1)}, bf16[4,2,2,4,160,376]{5,4,3,2,1,0:T(8,128)(2,1)S(1)}, u32[]{:S(2)}) %copy-start) | copy-done | bytes 7700504
  132.4 0.2 reshape.32
  132.6 0.4 slice.14
  133.1 0.1 copy.30
  133.2 0.6 reshape.33
  133.7 1.1 copy.24
  134.8 0.0 copy-start.1
  134.8 3.2 %copy-done.1 = bf16[4,2,2,4,160,376]{5,4,3,2,1,0:T(8,128)(2,1)S(1)} copy-done((bf16[4,2,2,4,160,376]{5,4,3,2,1,0:T(8,128)(2,1)S(1)}, bf16[4,2,2,4,160,376]{5,4,3,2,1,0:T(8,128)(2,1)}, u32[]{:S(2)}) %copy-start.1) | copy-done | bytes 7700504
  138.1 6.6 %shard_map.60 = f32[16,16,36,128]{3,2,1,0:T(8,128)S(1)} custom-call(bf16[4,2,2,4,160,376]{5,4,3,2,1,0:T(8,128)(2,1)S(1)} %copy-done.1, bf16[376,256]{1,0:T(8,128)(2,1)S(1)} %maximum_maximum_fusion.pattern_ref), custom_call_target="tpu_custom_call" | custom-call | tf_op jit(solution)/shard_map/pallas_call | solution.py:303
  144.6 3.0 %copy.25 = f32[256,36,128]{2,0,1:T(8,128)} copy(f32[256,36,128]{2,1,0:T(8,128)S(1)} %bitcast.18) | data formatting | bytes 9437184
  (5 shorter events, 0.1 us)
Async XLA Ops:
  129.3 3.1 %copy-start = (bf16[4,2,2,4,160,376]{5,4,3,2,1,0:T(8,128)(2,1)}, bf16[4,2,2,4,160,376]{5,4,3,2,1,0:T(8,128)(2,1)S(1)}, u32[]{:S(2)}) copy-start(bf16[4,2,2,4,160,376]{5,4,3,2,1,0:T(8,128)(2,1)S(1)} %get-tuple-element.5.weights_ref) | copy-start | bytes 23101444
  134.8 3.2 %copy-start.1 = (bf16[4,2,2,4,160,376]{5,4,3,2,1,0:T(8,128)(2,1)S(1)}, bf16[4,2,2,4,160,376]{5,4,3,2,1,0:T(8,128)(2,1)}, u32[]{:S(2)}) copy-start(bf16[4,2,2,4,160,376]{5,4,3,2,1,0:T(8,128)(2,1)} %copy-done) | copy-start | bytes 23101444

commit v3 on v2

--- a/solution.py
+++ b/solution.py
@@ -45,7 +45,7 @@
     return corr_real, corr_imag, 1.0 / noise_power
 
 
-def compute_part(part, volt_ref, mask_ref, count_ref, steer_ref, out_ref, mats):
+def compute_part(part, volt_ref, mask_ref, count_ref, steer_ref, out_ref, stage, mats):
     real_hi, real_lo, imag_hi, imag_lo = mats
     chans = real_hi.shape[0]
     ports = real_hi.shape[1]
@@ -91,7 +91,7 @@
         for inv in inverse_noise
     )
     states = lax.fori_loop(0, ITERS - 1, power_turn, states)
-    results = []
+    beam_rows = stage.shape[0] // chans
     for c in range(chans):
         mixed_real, mixed_imag = mix(c, states[c])
         total = jnp.sum(
@@ -102,13 +102,14 @@
         factor = lax.rsqrt(total / (2 * ports) + 1e-06) * inverse_noise[c]
         weight_real = (steer_real * mixed_real - steer_imag * mixed_imag) * factor
         weight_imag = (steer_real * mixed_imag + steer_imag * mixed_real) * factor
-        results.append(jnp.concatenate([weight_real, weight_imag], axis=1))
-    out_ref[part] = jnp.concatenate(results, axis=0).astype(jnp.bfloat16)
+        both = jnp.concatenate([weight_real, weight_imag], axis=1)
+        stage[c * beam_rows : (c + 1) * beam_rows] = both[:beam_rows]
+    out_ref[part] = stage[...].astype(jnp.bfloat16)
 
 
 def exchange_kernel(
     dims, blocks_ref, pick_ref, mask_ref, count_ref, gathered_ref, own_ref,
-    arrived, slots, partial, steer, real_hi, real_lo, imag_hi, imag_lo,
+    arrived, slots, partial, steer, stage, real_hi, real_lo, imag_hi, imag_lo,
     volt_send, volt_recv, steer_send, steer_recv,
     z_send, z_recv, x_send, x_recv, core_send, core_recv, place_sem,
 ):
@@ -183,28 +184,34 @@
             total = total + slots[base + d - 1].astype(jnp.float32)
         base += extent - 1
     steer[...] = total
-
-    def z_row(part):
-        return gathered_ref.at[part, my_core, my_x]
+    if parts > 1:
+        start_volts(1)
+
+    def slot(part, z):
+        return gathered_ref.at[part, my_core, my_x, z]
+
+    def to_x(part, source, z):
+        for d in range(1, width):
+            remote(
+                source, slot(part, z), x_send.at[part], x_recv.at[part],
+                device(my_z, lax.rem(my_x + d, width), my_core),
+            ).start()
 
     def start_z(part):
         for d in range(1, depth):
             remote(
-                own_ref.at[part], gathered_ref.at[part, my_core, my_x, my_z],
-                z_send.at[part], z_recv.at[part], device(lax.rem(my_z + d, depth), my_x, my_core),
+                own_ref.at[part], slot(part, my_z), z_send.at[part], z_recv.at[part, d],
+                device(lax.rem(my_z + d, depth), my_x, my_core),
             ).start()
-        pltpu.make_async_copy(
-            own_ref.at[part], gathered_ref.at[part, my_core, my_x, my_z], place_sem.at[part]
-        ).start()
+        to_x(part, own_ref.at[part], my_z)
+        pltpu.make_async_copy(own_ref.at[part], slot(part, my_z), place_sem.at[part]).start()
 
     def start_x(part):
         take(own_ref.at[part], place_sem.at[part])
-        take(gathered_ref.at[part, my_core, my_x, pl.ds(0, depth - 1)], z_recv.at[part])
-        for d in range(1, width):
-            remote(
-                z_row(part), z_row(part), x_send.at[part], x_recv.at[part],
-                device(my_z, lax.rem(my_x + d, width), my_core),
-            ).start()
+        for d in range(1, depth):
+            z = lax.rem(my_z + depth - d, depth)
+            take(slot(part, z), z_recv.at[part, d])
+            to_x(part, slot(part, z), z)
 
     def start_core(part):
         take(gathered_ref.at[part, my_core, pl.ds(0, width - 1)], x_recv.at[part])
@@ -219,12 +226,12 @@
     def _(part):
         take(arrived.at[part], volt_recv.at[part])
 
-        @pl.when(part + 1 < parts)
+        @pl.when(part + 2 < parts)
         def _():
-            start_volts(part + 1)
+            start_volts(part + 2)
 
         compute_part(
-            part, arrived, mask_ref, count_ref, steer, own_ref,
+            part, arrived, mask_ref, count_ref, steer, own_ref, stage,
             (real_hi, real_lo, imag_hi, imag_lo),
         )
         start_z(part)
@@ -251,12 +258,12 @@
         take(gathered_ref.at[part, pl.ds(0, cores - 1)], core_send.at[part])
 
 
-def exchange(dims, chans, blocks, pick, mask, count):
+def exchange(dims, chans, beam_rows, blocks, pick, mask, count):
     depth, width, cores = dims
     devices, parts, rows_dev, double = blocks.shape
     ports = double // 2
     beams2 = pick.shape[0]
-    rows = chans * beams2 // 2
+    rows = chans * beam_rows
     hops = depth + width + cores - 3
     bf16, dma = jnp.bfloat16, pltpu.SemaphoreType.DMA
     vmem = pl.BlockSpec(memory_space=pltpu.VMEM)
@@ -274,25 +281,27 @@
             pltpu.VMEM((hops, beams2, ports), bf16),
             pltpu.VMEM((3, beams2, ports), bf16),
             pltpu.VMEM((beams2, ports), jnp.float32),
+            pltpu.VMEM((rows, double), jnp.float32),
         ]
         + [pltpu.VMEM((chans, ports, ports), bf16)] * 4
         + [dma((parts,)), dma((parts,)), dma((hops,)), dma((hops,))]
-        + [dma((parts,))] * 7,
+        + [dma((parts,)), dma((parts, depth))] + [dma((parts,))] * 5,
         compiler_params=pltpu.CompilerParams(
-            collective_id=0, has_side_effects=True, vmem_limit_bytes=40 * 1024 * 1024
+            collective_id=0, has_side_effects=True, vmem_limit_bytes=56 * 1024 * 1024
         ),
     )(blocks, pick, mask, count)
 
 
-def map_kernel(beams, weights_ref, pattern_ref, out_ref):
+def map_kernel(weights_ref, pattern_ref, out_ref, power):
     parts, _, _, _, rows, double = weights_ref.shape
-    chans = out_ref.shape[1] // parts
-    pixels = pattern_ref.shape[1] // 2
+    beams, _, chans, pixels = out_ref.shape
+    stride = parts * rows // chans
     flat = weights_ref[:, 0, 0, 0].reshape(parts * rows, double)
     response = dot32(flat, pattern_ref[...])
     real, imag = response[:, :pixels], response[:, pixels:]
-    power = (real * real + imag * imag).reshape(parts * chans, rows // chans, pixels)
-    out_ref[0] = power[:, :beams]
+    power[...] = real * real + imag * imag
+    for b in range(beams):
+        out_ref[b, 0] = power[pl.ds(b, chans, stride=stride), :]
 
 
 def beam_power(dims, chans, gathered, patterns, beams):
@@ -300,10 +309,11 @@
     parts, _, _, _, rows, double = gathered.shape
     pixels = patterns.shape[1] // 2
     senders = depth * width * cores
+    per_dev = parts * chans
     return pl.pallas_call(
-        functools.partial(map_kernel, beams),
+        map_kernel,
         grid=(senders,),
-        out_shape=jax.ShapeDtypeStruct((senders, parts * chans, beams, pixels), jnp.float32),
+        out_shape=jax.ShapeDtypeStruct((beams, senders, per_dev, pixels), jnp.float32),
         in_specs=[
             pl.BlockSpec(
                 (parts, 1, 1, 1, rows, double),
@@ -311,8 +321,9 @@
             ),
             pl.BlockSpec((double, 2 * pixels), lambda i: (0, 0)),
         ],
-        out_specs=pl.BlockSpec((1, parts * chans, beams, pixels), lambda i: (i, 0, 0, 0)),
-        compiler_params=pltpu.CompilerParams(vmem_limit_bytes=32 * 1024 * 1024),
+        out_specs=pl.BlockSpec((beams, 1, per_dev, pixels), lambda i: (0, i, 0, 0)),
+        scratch_shapes=[pltpu.VMEM((parts * rows, pixels), jnp.float32)],
+        compiler_params=pltpu.CompilerParams(vmem_limit_bytes=56 * 1024 * 1024),
     )(gathered, patterns)
 
 
@@ -335,6 +346,7 @@
     parts = 4 if per_dev % 4 == 0 else 1
     chans = per_dev // parts
     dims = torus_dims(devices)
+    beam_rows = beams if (chans * beams) % 16 == 0 else padded
     total_time = samples_dev * devices
     off_span = max(4, total_time // 32)
     is_off = off_flags(jnp.arange(total_time, dtype=jnp.int32), off_starts, off_span)
@@ -355,12 +367,12 @@
         ],
         axis=0,
     )
-    gathered, own = exchange(dims, chans, blocks, picked, mask, count)
+    gathered, own = exchange(dims, chans, beam_rows, blocks, picked, mask, count)
     maps = beam_power(dims, chans, gathered, pattern_rows, beams)
-    own = own.reshape(per_dev, padded, 2, ports)[:, :beams].transpose(0, 2, 1, 3)
+    own = own.reshape(per_dev, beam_rows, 2, ports)[:, :beams].transpose(0, 2, 1, 3)
     return (
         own.reshape(per_dev, 2, beams * ports),
-        maps.reshape(channels, beams, pixels),
+        maps.reshape(beams, channels, pixels).transpose(1, 0, 2),
     )
 
 

time: 149 us -> 138 us (0.926)
  local copies, waits for them, and re-layouts: 27.2 us -> 16.4 us
    unnamed x9 -> x3, local copies, waits for them, and re-layouts: 19.8 us -> 9.9 us
    pallas_call x1, Pallas kernels: 110 us -> 103 us  [exchange(): pl.pallas_call(functools.partial(exchange_kernel, dims), out_shape=(jax.S...]
    pallas_call x1, Pallas kernels: 6.56 us -> 13.2 us  [beam_power(): pl.pallas_call(map_kernel, grid=(senders,), out_shape=jax.ShapeDtypeStruc...]
    reshape x1, local copies, waits for them, and re-layouts: 4.86 us -> 1.98 us  [on_device(): blocks = voltages.reshape(devices, parts, chans * samples_dev, 2 * ports)]
where the time goes in v3:
time: 138 us; the launch traced here: 137 us
  Pallas kernels  116 us (84%)
  local copies, waits for them, and re-layouts  16.4 us (12%)
  other arithmetic  2.72 us (2%)
  matrix products  1.7 us (1%)
    pallas_call x1, Pallas kernels, exchange(): pl.pallas_call(functools.partial(exchange_kernel, dims), out_shape=(jax.S...  103 us
    pallas_call x1, Pallas kernels, beam_power(): pl.pallas_call(map_kernel, grid=(senders,), out_shape=jax.ShapeDtypeStruc...  13.2 us
    unnamed x3, local copies, waits for them, and re-layouts  9.9 us

profile of v3, /device:TPU:29, one launch (start us, length us, event | category | flops | bytes accessed | tf_op | source)
XLA Modules:
  0.0 137.4 jit_solution(18075274085481614305)
XLA Ops:
  0.6 0.7 pad.4
  1.3 0.7 broadcast_add_fusion
  2.0 0.7 fusion.5
  2.7 0.6 convert_reduce_fusion
  3.3 1.2 broadcast_in_dim.5.count_ref
  4.5 1.7 %convolution_convert_fusion = bf16[40,2,188]{2,0,1:T(8,128)(2,1)} fusion(s32[128]{0:T(128)S(1)} %iota_add_fusion, s32[40]{0:T(128)S(1)} %pad.4, bf16[2,188,128]{2,0,1:T(2,128)(2,1)} %param.7), kind=kOutput, calls=%fused_computation | convolution fusion | flops 3870400 | bytes 127008 | tf_op jit(solution)/shard_map/rpx,bx->rbp/dot_general | solution.py:360
  6.2 0.9 copy.18
  7.2 0.7 maximum_maximum_fusion.pattern_ref
  7.9 0.7 broadcast_in_dim.4.mask_ref
  8.6 7.9 %copy.17 = bf16[256,8,2,188]{3,2,1,0:T(2,128)(2,1)S(1)} copy(bf16[256,8,2,188]{0,2,3,1:T(2,128)(2,1)} %param.4) | data formatting | bytes 3080192 | tf_op args[0]
  16.5 2.0 %reshape.30.blocks_ref = bf16[16,4,32,376]{3,2,1,0:T(8,128)(2,1)} reshape(bf16[256,8,2,188]{3,2,1,0:T(2,128)(2,1)S(1)} %copy.17) | data formatting | bytes 3080192 | tf_op jit(solution)/shard_map/reshape | solution.py:362
  18.5 102.8 %shard_map.59 = (bf16[4,2,2,4,144,376]{5,4,3,2,1,0:T(8,128)(2,1)}, bf16[4,144,376]{2,1,0:T(8,128)(2,1)}) custom-call(bf16[16,4,32,376]{3,2,1,0:T(8,128)(2,1)} %reshape.30.blocks_ref, bf16[80,188]{1,0:T(8,128)(2,1)} %bitcast.22, f32[128,188]{1,0:T(8,128)} %broadcast_in_dim.4.mask_ref, f32[1,188]{1,0:T(1,128)} %broadcast_in_dim.5.count_ref), custom_call_target="tpu_custom_call" | custom-call | tf_op jit(solution)/shard_map/pallas_call | solution.py:271
  121.3 1.2 reshape.32
  122.5 0.1 copy.26
  122.6 0.5 reshape.33
  123.1 1.1 copy.22
  124.2 13.2 %shard_map.60 = f32[36,16,16,128]{3,2,1,0:T(8,128)} custom-call(bf16[4,2,2,4,144,376]{5,4,3,2,1,0:T(8,128)(2,1)} %get-tuple-element.5.weights_ref, bf16[376,256]{1,0:T(8,128)(2,1)} %maximum_maximum_fusion.pattern_ref), custom_call_target="tpu_custom_call" | custom-call | tf_op jit(solution)/shard_map/pallas_call | solution.py:313
  (4 shorter events, 0.0 us)
